TPU v7x, 32 devices: a whole 2x2x4 slice. The times are simulated.
32 devices in a mesh: grp: 2 (over y), seq: 4 (over z), rep: 2 (over x), sub: 2 (over core).
Axes of the slice: x: 2, y: 2, z: 4, core: 2. Of those that a mesh axis runs over, the one named last changes fastest.
Arguments:
- prompt_q: bfloat16 [1024, 512], P(('grp', 'seq', 'rep'), 'sub'), parts along dimension 0, may hold values from -16 to 16
- prompt_kv: bfloat16 [1024, 256], P(('grp', 'seq', 'rep')), parts along dimension 0, may hold values from -6 to 6
- prompt_dout: bfloat16 [1024, 512], P(('grp', 'seq', 'rep'), 'sub'), parts along dimension 0, may hold values from -6 to 6
- resp_q: bfloat16 [8, 256, 512], P(('grp', 'rep', 'sub'), 'seq'), parts along dimension 0, may hold values from -16 to 16
- resp_kv: bfloat16 [8, 256, 256], P(('grp', 'rep', 'sub'), 'seq'), parts along dimension 0, may hold values from -6 to 6
- resp_dout: bfloat16 [8, 256, 512], P(('grp', 'rep', 'sub'), 'seq'), parts along dimension 0, may hold values from -6 to 6
- resp_lengths: int32 [8], P('grp'), parts along dimension 0, may hold values from 1 to 256, 640 in all
Outputs:
- prompt_out: bfloat16 [1024, 512], P(('grp', 'seq', 'rep'), 'sub'), parts along dimension 0
- resp_out: bfloat16 [8, 256, 512], P(('grp', 'rep', 'sub'), 'seq'), parts along dimension 0
- prompt_dq: bfloat16 [1024, 512], P(('grp', 'seq', 'rep'), 'sub'), parts along dimension 0
- resp_dq: bfloat16 [8, 256, 512], P(('grp', 'rep', 'sub'), 'seq'), parts along dimension 0
- prompt_dkv: bfloat16 [1024, 256], P(('grp', 'seq', 'rep')), parts along dimension 0
- resp_dkv: bfloat16 [8, 256, 256], P(('grp', 'rep', 'sub'), 'seq'), parts along dimension 0
There are 2 independent parts, one for each index of `grp`. A program takes and returns all parts, laid end to end along the dimension named above; each array names one. Nothing has to cross between parts.
Inputs may be any that keep to these rules, and one draw needn't show every extreme that they name: `resp_lengths`: the lengths sum to 640; the largest is 256.
All inputs are finite; a program needn't handle non-finite values.
Results may differ from a plain program's by a relative error of at most 0.0093.
Values may be sent and summed in bfloat16 or wider, within the bound.
A program may use at most 128 MiB of HBM per device.

v0:
```python
import jax
import jax.numpy as jnp
from jax import lax
from jax.sharding import PartitionSpec as P

floor_score = -1e30


def pick_block(key_count):
    for block_size in (512, 384, 256, 128):
        if key_count % block_size == 0:
            return block_size
    return key_count


def blocked(key_array, positions):
    block_size = pick_block(key_array.shape[0])
    block_count = key_array.shape[0] // block_size
    return (
        key_array.reshape(block_count, block_size, key_array.shape[1]),
        positions.reshape(block_count, block_size),
    )


def attend_set(queries, cotangent, query_pos, keep_rows, key_sets, score_scale):
    query_rows, head_count, head_dim = queries.shape

    def block_scores(key_block, positions):
        scores = (
            jnp.einsum(
                "qhe,ke->hqk", queries, key_block[:, :head_dim], preferred_element_type=jnp.float32
            )
            * score_scale
        )
        allowed = (positions[None, :] <= query_pos[:, None])[None]
        return (scores, allowed)

    def stats_step(state_pair, key_item):
        row_top, row_total = state_pair
        key_block, positions = key_item
        scores, allowed = block_scores(key_block, positions)
        new_top = jnp.maximum(row_top, jnp.max(jnp.where(allowed, scores, floor_score), axis=2))
        row_total = row_total * jnp.exp(row_top - new_top) + jnp.sum(
            jnp.where(allowed, jnp.exp(scores - new_top[:, :, None]), 0.0), axis=2
        )
        return ((new_top, row_total), None)

    state_pair = (
        jnp.full((head_count, query_rows), floor_score, jnp.float32),
        jnp.zeros((head_count, query_rows), jnp.float32),
    )
    for key_set in key_sets:
        state_pair, unused = lax.scan(stats_step, state_pair, key_set)
    row_top, row_total = state_pair

    def prob_of(scores, allowed):
        return (
            jnp.where(allowed, jnp.exp(scores - row_top[:, :, None]), 0.0) / row_total[:, :, None]
        )

    def output_step(accum_out, key_item):
        key_block, positions = key_item
        scores, allowed = block_scores(key_block, positions)
        weights = prob_of(scores, allowed).astype(jnp.bfloat16) * keep_rows
        accum_out = accum_out + jnp.einsum(
            "hqk,ke->qhe", weights, key_block[:, head_dim:], preferred_element_type=jnp.float32
        )
        return (accum_out, None)

    output = jnp.zeros((query_rows, head_count, head_dim), jnp.float32)
    for key_set in key_sets:
        output, unused = lax.scan(output_step, output, key_set)
    row_delta = jnp.transpose(jnp.sum(cotangent.astype(jnp.float32) * output, axis=2))

    def grad_step(accum_grad, key_item):
        key_block, positions = key_item
        scores, allowed = block_scores(key_block, positions)
        prob_f32 = prob_of(scores, allowed)
        weights = prob_f32.astype(jnp.bfloat16) * keep_rows
        grad_prob = jnp.einsum(
            "qhe,ke->hqk", cotangent, key_block[:, head_dim:], preferred_element_type=jnp.float32
        )
        dscore = (prob_f32 * (grad_prob - row_delta[:, :, None])).astype(jnp.bfloat16) * keep_rows
        accum_grad = accum_grad + jnp.einsum(
            "hqk,ke->qhe", dscore, key_block[:, :head_dim], preferred_element_type=jnp.float32
        )
        key_grad = (
            jnp.einsum("hqk,qhe->ke", dscore, queries, preferred_element_type=jnp.float32)
            * score_scale
        )
        dvalue = jnp.einsum("hqk,qhe->ke", weights, cotangent, preferred_element_type=jnp.float32)
        return (accum_grad, jnp.concatenate([key_grad, dvalue], axis=1))

    dquery = jnp.zeros((query_rows, head_count, head_dim), jnp.float32)
    key_grads = []
    for key_set in key_sets:
        dquery, part_grad = lax.scan(grad_step, dquery, key_set)
        key_grads.append(part_grad.reshape(-1, 2 * head_dim))
    return (output, dquery * score_scale, key_grads)


def shards(prompt_q, prompt_kv, prompt_dout, resp_q, resp_kv, resp_dout, resp_lengths):
    prompt_rows, prompt_width = prompt_q.shape
    head_dim = prompt_kv.shape[1] // 2
    prompt_heads = prompt_width // head_dim
    query_width = resp_q.shape[2]
    head_count = query_width // head_dim
    score_scale = head_dim ** (-0.5)
    total_prompt = prompt_rows * lax.axis_size(("seq", "rep"))
    resp_rows = resp_q.shape[1]
    seq_count = lax.axis_size("seq")
    longest = resp_rows * seq_count
    prompt_start = lax.axis_index(("seq", "rep")) * prompt_rows
    member = lax.axis_index(("rep", "sub"))
    resp_start = lax.axis_index("seq") * resp_rows
    slot_ids = jnp.arange(resp_lengths.shape[0], dtype=jnp.int32)
    length = jnp.sum(jnp.where(slot_ids == member, resp_lengths, 0))
    prompt_keys = lax.all_gather(prompt_kv, ("seq", "rep"), axis=0, tiled=True)
    own_keys = lax.all_gather(resp_kv, "seq", axis=1, tiled=True)[0]
    prompt_set = blocked(prompt_keys, jnp.arange(total_prompt, dtype=jnp.int32))
    own_set = blocked(own_keys, total_prompt + jnp.arange(longest, dtype=jnp.int32))
    p_queries = prompt_q.reshape(prompt_rows, prompt_heads, head_dim)
    p_cotan = prompt_dout.reshape(prompt_rows, prompt_heads, head_dim)
    p_pos = prompt_start + jnp.arange(prompt_rows, dtype=jnp.int32)
    p_keep = jnp.ones((1, prompt_rows, 1), jnp.bfloat16)
    p_output, p_dquery, p_grads = attend_set(
        p_queries, p_cotan, p_pos, p_keep, [prompt_set], score_scale
    )
    r_queries = resp_q[0].reshape(resp_rows, head_count, head_dim)
    r_cotan = resp_dout[0].reshape(resp_rows, head_count, head_dim)
    places = resp_start + jnp.arange(resp_rows, dtype=jnp.int32)
    r_keep = (places < length).astype(jnp.bfloat16)[None, :, None]
    r_output, r_dquery, r_grads = attend_set(
        r_queries, r_cotan, total_prompt + places, r_keep, [prompt_set, own_set], score_scale
    )
    prompt_part = p_grads[0] + r_grads[0]
    resp_part = r_grads[1]
    pair_count = lax.axis_size(("seq", "rep"))
    grouped = prompt_part.reshape(pair_count, prompt_rows, 2 * head_dim)
    arrived = lax.all_to_all(grouped, ("seq", "rep"), split_axis=0, concat_axis=0, tiled=True)
    pair_rows = jnp.sum(arrived, axis=0)
    prompt_grad = lax.psum(pair_rows, "sub")
    arrived_resp = lax.all_to_all(
        resp_part.reshape(seq_count, resp_rows, 2 * head_dim),
        "seq",
        split_axis=0,
        concat_axis=0,
        tiled=True,
    )
    resp_grad = jnp.sum(arrived_resp, axis=0)
    prompt_out = p_output.reshape(prompt_rows, prompt_width).astype(jnp.bfloat16)
    prompt_dq = p_dquery.reshape(prompt_rows, prompt_width).astype(jnp.bfloat16)
    resp_out = r_output.reshape(1, resp_rows, query_width).astype(jnp.bfloat16)
    resp_dq = r_dquery.reshape(1, resp_rows, query_width).astype(jnp.bfloat16)
    return (
        prompt_out,
        resp_out,
        prompt_dq,
        resp_dq,
        prompt_grad.astype(jnp.bfloat16),
        resp_grad[None].astype(jnp.bfloat16),
    )


def solution(mesh):
    placed = (
        P(("grp", "seq", "rep"), "sub"),
        P(("grp", "seq", "rep"), None),
        P(("grp", "seq", "rep"), "sub"),
        P(("grp", "rep", "sub"), "seq", None),
        P(("grp", "rep", "sub"), "seq", None),
        P(("grp", "rep", "sub"), "seq", None),
        P("grp"),
    )
    return jax.shard_map(
        shards,
        mesh=mesh,
        in_specs=placed,
        out_specs=(
            P(("grp", "seq", "rep"), "sub"),
            P(("grp", "rep", "sub"), "seq", None),
            P(("grp", "seq", "rep"), "sub"),
            P(("grp", "rep", "sub"), "seq", None),
            P(("grp", "seq", "rep"), None),
            P(("grp", "rep", "sub"), "seq", None),
        ),
        check_vma=False,
    )
```

profile of v0, /device:TPU:1, one launch (start us, length us, event | category | flops | bytes accessed | tf_op | source)
XLA Modules:
  0.0 86.9 jit_solution(13082078292845571912)
XLA Ops:
  0.6 0.0 copy-start
  0.7 26.1 %all_gather.6 = bf16[512,256]{1,0:T(8,128)(2,1)S(1)} all-gather(bf16[64,256]{1,0:T(8,128)(2,1)} %param.8), channel_id=1, replica_groups=mesh['grp'=2,'seq'=4,'rep'=2,'sub'=2] {'seq','rep'}, dimensions={0}, use_global_device_ids=true | all-gather | bytes 294912 | tf_op jit(solution)/shard_map/all_gather | solution.py:118
  26.8 0.6 fusion.47
  27.4 0.6 compare_convert_fusion
  28.1 0.1 iota_compare_fusion
  28.2 0.1 broadcast_compare_fusion
  28.3 0.7 copy-done.3
  29.0 10.5 %all_gather.7 = bf16[1,256,256]{2,1,0:T(8,128)(2,1)S(1)} all-gather(bf16[1,64,256]{2,1,0:T(8,128)(2,1)S(1)} %copy-done.3), channel_id=1, replica_groups=mesh['grp'=2,'seq'=4,'rep'=2,'sub'=2] {'seq'}, dimensions={1}, use_global_device_ids=true | all-gather | bytes 163840 | tf_op jit(solution)/shard_map/all_gather | solution.py:119
  39.5 0.3 select_reduce_fusion.2
  39.8 0.3 select_reduce_fusion.1
  40.1 0.2 fusion.26
  40.3 0.2 select_reduce_fusion
  40.6 0.2 convert_multiply_fusion.1
  40.8 0.2 convert_multiply_fusion
  41.0 0.6 copy-done.2
  41.6 0.2 fusion.30
  41.8 0.2 convolution_bitcast_fusion.7
  42.0 0.3 multiply_reduce_fusion
  42.3 0.2 fusion.15
  42.5 0.2 fusion.18
  42.8 0.8 copy.38
  43.6 3.4 %all-to-all-start.1 = ((f32[4,64,256]{2,1,0:T(8,128)}), f32[4,64,256]{2,1,0:T(8,128)S(1)}, u32[]{:S(2)}, u32[]{:S(2)}) async-start(f32[4,64,256]{2,1,0:T(8,128)} %bitcast.24), calls=%async_computation.1 | async-start | bytes 524288 | tf_op jit(solution)/shard_map/all_to_all | solution.py:143
  47.0 0.3 fusion.10
  47.4 0.1 iota_compare_fusion.1
  47.4 0.6 copy-done.4
  48.1 0.3 select_reduce_fusion.3
  48.4 0.2 fusion.24
  48.6 0.3 multiply_reduce_fusion.1
  48.9 0.3 convolution_bitcast_fusion.3
  49.2 0.2 fusion.13
  49.4 0.2 fusion.12
  49.7 0.2 convolution_bitcast_fusion.1
  49.9 0.2 fusion.11
  50.1 0.1 maximum_add_fusion
  50.2 1.0 %copy.35 = f32[512,256]{1,0:T(8,128)} copy(f32[512,256]{0,1:T(8,128)S(1)} %maximum_add_fusion) | data formatting | bytes 1048576 | tf_op jit(solution)/shard_map/add | solution.py:136
  51.2 1.4 %all-to-all-done.1 = f32[4,64,256]{2,1,0:T(8,128)S(1)} async-done(((f32[4,64,256]{2,1,0:T(8,128)}), f32[4,64,256]{2,1,0:T(8,128)S(1)}, u32[]{:S(2)}, u32[]{:S(2)}) %all-to-all-start.1) | async-done | bytes 262176 | tf_op jit(solution)/shard_map/all_to_all | solution.py:143
  52.6 4.7 %all-to-all-start = ((f32[8,64,256]{2,1,0:T(8,128)}), f32[8,64,256]{2,1,0:T(8,128)S(1)}, u32[]{:S(2)}, u32[]{:S(2)}) async-start(f32[8,64,256]{2,1,0:T(8,128)} %bitcast.21), calls=%async_computation | async-start | bytes 1048576 | tf_op jit(solution)/shard_map/all_to_all | solution.py:140
  57.4 0.1 copy.23
  57.4 0.7 convert_element_type.113
  58.1 0.2 fusion.29
  58.3 0.2 fusion.20
  58.5 0.1 copy.30
  58.5 0.7 convert_element_type.124
  59.2 0.2 fusion.22
  59.4 0.6 copy_bitcast_fusion
  60.0 0.6 reduce_sum.82
  60.6 8.3 %all-to-all-done = f32[8,64,256]{2,1,0:T(8,128)S(1)} async-done(((f32[8,64,256]{2,1,0:T(8,128)}), f32[8,64,256]{2,1,0:T(8,128)S(1)}, u32[]{:S(2)}, u32[]{:S(2)}) %all-to-all-start) | async-done | bytes 524320 | tf_op jit(solution)/shard_map/all_to_all | solution.py:140
  69.0 17.9 %psum.7 = bf16[64,256]{1,0:T(8,128)(2,1)} all-reduce(f32[64,256]{1,0:T(8,128)S(1)} %reduce_sum.81), channel_id=1, replica_groups=mesh['grp'=2,'seq'=4,'rep'=2,'sub'=2] {'sub'}, use_global_device_ids=true, to_apply=%region_10.11 | all-reduce | flops 16384 | bytes 98304 | tf_op jit(solution)/shard_map/psum | solution.py:142
  (19 shorter events, 0.2 us)
Async XLA Ops:
  0.6 48.0 %copy-start = (bf16[64,256]{1,0:T(8,128)(2,1)S(1)}, bf16[64,256]{1,0:T(8,128)(2,1)}, u32[]{:S(2)}) copy-start(bf16[64,256]{1,0:T(8,128)(2,1)} %param.9) | copy-start | bytes 98308
  0.7 26.1 %copy-start.5 = (s32[4]{0:T(128)S(1)}, s32[4]{0:T(128)}, u32[]{:S(2)}) copy-start(s32[4]{0:T(128)} %param.13) | copy-start | bytes 52
  26.8 1.5 %copy-start.1 = (bf16[1,64,512]{2,1,0:T(8,128)(2,1)S(1)}, bf16[1,64,512]{2,1,0:T(8,128)(2,1)}, u32[]{:S(2)}) copy-start(bf16[1,64,512]{2,1,0:T(8,128)(2,1)} %param.10) | copy-start | bytes 196612
  28.3 0.8 copy-start.3
  40.7 0.8 copy-start.2
  43.6 9.0 %all-to-all-start.1 = ((f32[4,64,256]{2,1,0:T(8,128)}), f32[4,64,256]{2,1,0:T(8,128)S(1)}, u32[]{:S(2)}, u32[]{:S(2)}) async-start(f32[4,64,256]{2,1,0:T(8,128)} %bitcast.24), calls=%async_computation.1 | async-start | bytes 524288 | tf_op jit(solution)/shard_map/all_to_all | solution.py:143
  47.3 0.8 copy-start.4
  52.6 16.3 %all-to-all-start = ((f32[8,64,256]{2,1,0:T(8,128)}), f32[8,64,256]{2,1,0:T(8,128)S(1)}, u32[]{:S(2)}, u32[]{:S(2)}) async-start(f32[8,64,256]{2,1,0:T(8,128)} %bitcast.21), calls=%async_computation | async-start | bytes 1048576 | tf_op jit(solution)/shard_map/all_to_all | solution.py:140
where the time goes:
time: 87.6 us; the launch traced here: 86.9 us
  blocking collectives  54.4 us (62%)
  waiting for transfers between devices  9.72 us (11%)
  starting transfers between devices  8.15 us (9%)
  local copies, waits for them, and re-layouts  5.94 us (7%)
  matrix products  4.33 us (5%)
  other arithmetic  3.35 us (4%)
  between operations  0.96 us (1%)
    all_gather x1, blocking collectives, shards(): prompt_keys = lax.all_gather(prompt_kv, ('seq', 'rep'), axis=0, tiled=True)  26.1 us
    psum x1, blocking collectives, shards(): prompt_grad = lax.psum(pair_rows, 'sub')  17.9 us
    all_gather x1, blocking collectives, shards(): own_keys = lax.all_gather(resp_kv, 'seq', axis=1, tiled=True)[0]  10.5 us
    all_to_all x1, waiting for transfers between devices, shards(): lax.all_to_all(grouped, ('seq', 'rep'), split_axis=0, concat_axis=0, tile...  8.32 us
    all_to_all x1, starting transfers between devices, shards(): lax.all_to_all(grouped, ('seq', 'rep'), split_axis=0, concat_axis=0, tile...  4.75 us
    all_to_all x1, starting transfers between devices, shards(): lax.all_to_all(resp_part.reshape(seq_count, resp_rows, 2 * head_dim), 'se...  3.4 us
    unnamed x12, local copies, waits for them, and re-layouts  2 us
  transfers between devices with their start and end apart: 2, of which 2 were waited for; matrix products, arithmetic and copies ran while one was open for 8% of the time, Pallas kernels for 0%

commit v1 on v0

v1 whole, which is shorter than its diff:
```python
import functools
import math

import jax
import jax.numpy as jnp
from jax import lax
from jax.experimental import pallas as pl
from jax.experimental.pallas import tpu as pltpu
from jax.sharding import PartitionSpec as P

MESH = pl.DeviceIdType.MESH
NT = (((1,), (1,)), ((), ()))
NN = (((1,), (0,)), ((), ()))
TN = (((0,), (0,)), ((), ()))
floor_score = -1e30
f32, bf16 = jnp.float32, jnp.bfloat16


def dot(a, b, dims):
    return lax.dot_general(a, b, dims, preferred_element_type=f32)


def loop(low, high, body):
    if high - low <= 8:
        for i in range(low, high):
            body(i)
    else:
        lax.fori_loop(low, high, lambda i, c: (body(i), c)[1], 0)


def fold(count, body, carry):
    if count <= 4:
        for i in range(count):
            carry = body(i, carry)
        return carry
    return lax.fori_loop(0, count, body, carry)


def kernel(
    nz, nx, ns, lens, pq, pkv, pdo, rq, rkv, rdo, po, ro, pdq, rdq, pdkv, rdkv,
    pk, rk, qa, da, sp, gp, so, go, wp, dp, wo, do, away, got, mine, rs, oway, rr, fin,
    g_send, g_recv, f_send, f_recv, r_send, r_recv, p_sem, s_send, s_recv, q_send, q_recv, e_sem,
):
    n = nz * nx
    rows, kvw = pkv.shape
    e = kvw // 2
    half = rows // 2
    z, x, h = lax.axis_index("seq"), lax.axis_index("rep"), lax.axis_index("sub")
    me = z * nx + x
    sib = {"sub": 1 - h}
    p_heads = pq.shape[1] // e
    r_heads = rq.shape[2] // e
    r_rows = rq.shape[1]
    rc = r_heads * r_rows
    pc = p_heads * rows
    scale = 1.0 / math.sqrt(e)
    scale2 = scale * math.log2(math.e)
    bk = sp.shape[1]
    cpb = bk // half
    nb2 = sp.shape[0]
    nb = nb2 // 2
    bo = so.shape[1]
    zpb = bo // r_rows
    no = so.shape[0]

    def chip(c):
        return {"seq": c // nx, "rep": c % nx}

    def copy(src, dst, send, recv, to):
        return pltpu.make_async_remote_copy(
            src_ref=src, dst_ref=dst, send_sem=send, recv_sem=recv, device_id=to, device_id_type=MESH
        )

    barrier = pltpu.get_barrier_semaphore()

    def greet(d):
        pl.semaphore_signal(barrier, inc=1, device_id=chip((me + d) % n), device_id_type=MESH)

    loop(1, n, greet)
    pl.semaphore_signal(barrier, inc=1, device_id=sib, device_id_type=MESH)

    for k in range(2):
        pk[k * n + me] = pkv[k * half : (k + 1) * half, :]
    rk[z] = rkv[0]

    def blank(i):
        @pl.when(i > z)
        def _():
            rk[i] = jnp.zeros(rk.shape[1:], bf16)

    loop(0, nz, blank)
    for k in range(r_heads):
        qa[k * r_rows : (k + 1) * r_rows, :] = rq[0, :, k * e : (k + 1) * e]
        da[k * r_rows : (k + 1) * r_rows, :] = rdo[0, :, k * e : (k + 1) * e]
    for k in range(p_heads):
        qa[rc + k * rows : rc + (k + 1) * rows, :] = pq[:, k * e : (k + 1) * e]
        da[rc + k * rows : rc + (k + 1) * rows, :] = pdo[:, k * e : (k + 1) * e]

    pl.semaphore_wait(barrier, n)

    def gather(c, src):
        return copy(pk.at[h * n + src], pk.at[h * n + src], g_send.at[c], g_recv.at[src], chip(c))

    def pass_on(c, k):
        return copy(pk.at[k * n + c], pk.at[k * n + c], f_send.at[c], f_recv.at[c], sib)

    def resp(to, src):
        return copy(rk.at[src], rk.at[src], r_send.at[to], r_recv.at[src], {"seq": to})

    loop(1, n, lambda d: gather((me + d) % n, me).start())

    def resp_start(i):
        @pl.when(i > z)
        def _():
            resp(i, z).start()

    loop(0, nz, resp_start)

    def forward(d):
        c = (me + n - d) % n
        gather(c, c).wait_recv()
        pass_on(c, h).start()

    loop(1, n, forward)

    def resp_wait(i):
        @pl.when(i < z)
        def _():
            resp(i, i).wait_recv()

    loop(0, nz, resp_wait)

    def own_scores(i, top):
        kv = rk[pl.ds(i * zpb, zpb)].reshape(bo, kvw)
        s = dot(kv[:, :e], qa[:rc], NT) * scale2
        key = i * bo + lax.broadcasted_iota(jnp.int32, (bo, rc), 0)
        at = z * r_rows + lax.broadcasted_iota(jnp.int32, (bo, rc), 1) % r_rows
        s = jnp.where(key <= at, s, floor_score)
        so[i] = s
        go[i] = dot(kv[:, e:], da[:rc], NT)
        return jnp.maximum(top, jnp.max(s, axis=0, keepdims=True))

    top_r = fold(no, own_scores, jnp.full((1, rc), floor_score, f32))

    loop(1, n, lambda d: pass_on((me + d) % n, 1 - h).wait_recv())

    def scores(i, tops):
        top_r, top_p = tops
        kv = pk[pl.ds(i * cpb, cpb)].reshape(bk, kvw)
        s = dot(kv[:, :e], qa[...], NT) * scale2
        place = lax.broadcasted_iota(jnp.int32, (bk, pc), 0)
        key = ((i % nb) * cpb + place // half) * rows + (i // nb) * half + place % half
        at = me * rows + lax.broadcasted_iota(jnp.int32, (bk, pc), 1) % rows
        s_r = s[:, :rc]
        s_p = jnp.where(key <= at, s[:, rc:], floor_score)
        sp[i, :, :rc] = s_r
        sp[i, :, rc:] = s_p
        gp[i] = dot(kv[:, e:], da[...], NT)
        return (
            jnp.maximum(top_r, jnp.max(s_r, axis=0, keepdims=True)),
            jnp.maximum(top_p, jnp.max(s_p, axis=0, keepdims=True)),
        )

    top_r, top_p = fold(nb2, scores, (top_r, jnp.full((1, pc), floor_score, f32)))
    top = jnp.concatenate([top_r, top_p], axis=1)

    def own_exp(i, sums):
        total, delta = sums
        ex = jnp.exp2(so[i] - top_r)
        so[i] = ex
        return (
            total + jnp.sum(ex, axis=0, keepdims=True),
            delta + jnp.sum(ex * go[i], axis=0, keepdims=True),
        )

    def all_exp(i, sums):
        total, delta = sums
        ex = jnp.exp2(sp[i] - top)
        sp[i] = ex
        return (
            total + jnp.sum(ex, axis=0, keepdims=True),
            delta + jnp.sum(ex * gp[i], axis=0, keepdims=True),
        )

    zero_r, zero_a = jnp.zeros((1, rc), f32), jnp.zeros((1, rc + pc), f32)
    total_o, delta_o = fold(no, own_exp, (zero_r, zero_r))
    total, delta = fold(nb2, all_exp, (zero_a, zero_a))
    total_r = total[:, :rc] + total_o
    total = jnp.concatenate([total_r, total[:, rc:]], axis=1)
    delta = jnp.concatenate([delta[:, :rc] + delta_o, delta[:, rc:]], axis=1) / total
    length = lens[x * ns + h]
    column = lax.broadcasted_iota(jnp.int32, (1, rc + pc), 1)
    live = jnp.logical_or(column >= rc, z * r_rows + column % r_rows < length)
    share = jnp.where(live, 1.0 / total, 0.0)

    def weigh(i, carry):
        prob = sp[i] * share
        wp[i] = prob.astype(bf16)
        dp[i] = (prob * (gp[i] - delta)).astype(bf16)
        return carry

    def own_weigh(i, carry):
        prob = so[i] * share[:, :rc]
        wo[i] = prob.astype(bf16)
        do[i] = (prob * (go[i] - delta[:, :rc])).astype(bf16)
        return carry

    fold(nb2, weigh, 0)
    fold(no, own_weigh, 0)

    def part(k, b):
        dk = dot(dp[k * nb + b], qa[...], NN) * scale
        dv = dot(wp[k * nb + b], da[...], NN)
        return jnp.concatenate([dk, dv], axis=1)

    def sib_part(b, carry):
        away[b] = part(1 - h, b).astype(bf16)
        return carry

    fold(nb, sib_part, 0)
    pair = copy(away, got, p_sem.at[0], p_sem.at[1], sib)
    pair.start()

    def own_part(i, carry):
        dk = dot(do[i], qa[:rc], NN) * scale
        dv = dot(wo[i], da[:rc], NN)
        both = jnp.concatenate([dk, dv], axis=1).astype(bf16)
        oway[pl.ds(i * zpb, zpb)] = both.reshape(zpb, r_rows, kvw)
        return carry

    fold(no, own_part, 0)

    def back(to, src):
        return copy(oway.at[to], rr.at[src], q_send.at[to], q_recv.at[src], {"seq": to})

    def back_start(i):
        @pl.when(i < z)
        def _():
            back(i, z).start()

    loop(0, nz, back_start)

    def my_part(b, carry):
        mine[b] = part(h, b)
        return carry

    fold(nb, my_part, 0)
    pair.wait_recv()

    def add(b, carry):
        both = (mine[b] + got[b].astype(f32)).astype(bf16)
        rs[0, pl.ds(b * cpb, cpb)] = both.reshape(cpb, half, kvw)
        return carry

    fold(nb, add, 0)

    def scatter(c, src):
        return copy(rs.at[0, c], rs.at[1, src], s_send.at[c], s_recv.at[src], chip(c))

    loop(1, n, lambda d: scatter((me + d) % n, me).start())
    rs[1, me] = rs[0, me]

    def out_own(i, carry):
        o, q = carry
        kv = rk[pl.ds(i * zpb, zpb)].reshape(bo, kvw)
        return o + dot(kv[:, e:], wo[i], TN), q + dot(kv[:, :e], do[i], TN)

    def out_all(i, carry):
        o, q = carry
        kv = pk[pl.ds(i * cpb, cpb)].reshape(bk, kvw)
        return o + dot(kv[:, e:], wp[i], TN), q + dot(kv[:, :e], dp[i], TN)

    zo, za = jnp.zeros((e, rc), f32), jnp.zeros((e, rc + pc), f32)
    o_o, q_o = fold(no, out_own, (zo, zo))
    o_a, q_a = fold(nb2, out_all, (za, za))
    o_r = jnp.transpose(o_a[:, :rc] + o_o)
    o_p = jnp.transpose(o_a[:, rc:])
    q_r = jnp.transpose((q_a[:, :rc] + q_o) * scale)
    q_p = jnp.transpose(q_a[:, rc:] * scale)
    for k in range(r_heads):
        ro[0, :, k * e : (k + 1) * e] = o_r[k * r_rows : (k + 1) * r_rows].astype(bf16)
        rdq[0, :, k * e : (k + 1) * e] = q_r[k * r_rows : (k + 1) * r_rows].astype(bf16)
    for k in range(p_heads):
        po[:, k * e : (k + 1) * e] = o_p[k * rows : (k + 1) * rows].astype(bf16)
        pdq[:, k * e : (k + 1) * e] = q_p[k * rows : (k + 1) * rows].astype(bf16)

    loop(1, n, lambda d: scatter((me + n - d) % n, (me + n - d) % n).wait_recv())
    summed = lax.fori_loop(
        0, n, lambda c, t: t + rs[1, c].astype(f32), jnp.zeros((half, kvw), f32), unroll=min(n, 8)
    )
    fin[h] = summed.astype(bf16)
    last = copy(fin.at[h], fin.at[h], e_sem.at[0], e_sem.at[1], sib)
    last.start()

    def back_wait(i):
        @pl.when(i > z)
        def _():
            back(i, i).wait_recv()

    loop(0, nz, back_wait)
    rr[z] = oway[z]
    own_sum = lax.fori_loop(
        0,
        nz,
        lambda c, t: t + jnp.where(c >= z, rr[c].astype(f32), 0.0),
        jnp.zeros((r_rows, kvw), f32),
        unroll=min(nz, 8),
    )
    rdkv[0] = own_sum.astype(bf16)
    copy(fin.at[1 - h], fin.at[1 - h], e_sem.at[0], e_sem.at[1], sib).wait_recv()
    pdkv[:half, :] = fin[0]
    pdkv[half:, :] = fin[1]

    loop(1, n, lambda d: gather((me + d) % n, me).wait_send())
    loop(1, n, lambda d: pass_on((me + d) % n, h).wait_send())
    loop(1, n, lambda d: scatter((me + d) % n, me).wait_send())

    def sent(i):
        @pl.when(i > z)
        def _():
            resp(i, z).wait_send()

        @pl.when(i < z)
        def _():
            back(i, z).wait_send()

    loop(0, nz, sent)
    pair.wait_send()
    last.wait_send()


def shards(nz, nx, ns, prompt_q, prompt_kv, prompt_dout, resp_q, resp_kv, resp_dout, resp_lengths):
    n = nz * nx
    rows, kvw = prompt_kv.shape
    e = kvw // 2
    half = rows // 2
    r_rows = resp_q.shape[1]
    rc = resp_q.shape[2] // e * r_rows
    qc = rc + prompt_q.shape[1] // e * rows
    cpb = math.gcd(n, 8)
    bk = cpb * half
    nb2 = 2 * n // cpb
    zpb = math.gcd(nz, 4)
    bo = zpb * r_rows
    no = nz // zpb
    vmem = pl.BlockSpec(memory_space=pltpu.VMEM)
    scratch = [
        ((2 * n, half, kvw), bf16),
        ((nz, r_rows, kvw), bf16),
        ((qc, e), bf16),
        ((qc, e), bf16),
        ((nb2, bk, qc), f32),
        ((nb2, bk, qc), f32),
        ((no, bo, rc), f32),
        ((no, bo, rc), f32),
        ((nb2, bk, qc), bf16),
        ((nb2, bk, qc), bf16),
        ((no, bo, rc), bf16),
        ((no, bo, rc), bf16),
        ((nb2 // 2, bk, kvw), bf16),
        ((nb2 // 2, bk, kvw), bf16),
        ((nb2 // 2, bk, kvw), f32),
        ((2, n, half, kvw), bf16),
        ((nz, r_rows, kvw), bf16),
        ((nz, r_rows, kvw), bf16),
        ((2, half, kvw), bf16),
    ]
    room = sum(math.prod(s) * jnp.dtype(t).itemsize for s, t in scratch)
    dma = pltpu.SemaphoreType.DMA
    sems = [dma((k,)) for k in (n, n, n, n, nz, nz, 2, n, n, nz, nz, 2)]
    like = jax.ShapeDtypeStruct
    return pl.pallas_call(
        functools.partial(kernel, nz, nx, ns),
        out_shape=[
            like(a.shape, bf16)
            for a in (prompt_q, resp_q, prompt_q, resp_q, prompt_kv, resp_kv)
        ],
        in_specs=[pl.BlockSpec(memory_space=pltpu.SMEM)] + [vmem] * 6,
        out_specs=[vmem] * 6,
        scratch_shapes=[pltpu.VMEM(s, t) for s, t in scratch] + sems,
        compiler_params=pltpu.CompilerParams(
            collective_id=0, has_side_effects=True, vmem_limit_bytes=room + 8 * 2**20
        ),
    )(resp_lengths, prompt_q, prompt_kv, prompt_dout, resp_q, resp_kv, resp_dout)


def solution(mesh):
    prompt = P(("grp", "seq", "rep"), "sub")
    prompt_kv = P(("grp", "seq", "rep"), None)
    resp = P(("grp", "rep", "sub"), "seq", None)
    sizes = (mesh.shape["seq"], mesh.shape["rep"], mesh.shape["sub"])
    return jax.shard_map(
        functools.partial(shards, *sizes),
        mesh=mesh,
        in_specs=(prompt, prompt_kv, prompt, resp, resp, resp, P("grp")),
        out_specs=(prompt, resp, prompt, resp, prompt_kv, resp),
        check_vma=False,
    )
```

time: 87.6 us -> 33.3 us (0.38)
  blocking collectives: 54.4 us -> 0 us
  Pallas kernels: 0 us -> 23 us
  waiting for transfers between devices: 9.72 us -> 0 us
  starting transfers between devices: 8.15 us -> 0 us
  matrix products: 4.33 us -> 0 us
  other arithmetic: 3.35 us -> 0 us
  local copies, waits for them, and re-layouts: 5.94 us -> 9.07 us
    all_gather x2 -> x0, blocking collectives: 36.6 us -> none  [the longest x1 26.1 us: shards(): prompt_keys = lax.all_gather(prompt_kv, ('seq', 'rep'), axis=0, tiled=True)]
    pallas_call x0 -> x1, Pallas kernels: none -> 23 us  [shards(): pl.pallas_call(functools.partial(kernel, nz, nx, ns), out_shape=[like(a.s...]
    psum x1 -> x0, blocking collectives: 17.9 us -> none  [shards(): prompt_grad = lax.psum(pair_rows, 'sub')]
    all_to_all x2 -> x0, waiting for transfers between devices: 9.72 us -> none  [the longest x1 8.32 us: shards(): lax.all_to_all(grouped, ('seq', 'rep'), split_axis=0, concat_axis=0, tile...]
    all_to_all x2 -> x0, starting transfers between devices: 8.15 us -> none  [the longest x1 4.75 us: shards(): lax.all_to_all(grouped, ('seq', 'rep'), split_axis=0, concat_axis=0, tile...]
    unnamed x12 -> x20, local copies, waits for them, and re-layouts: 2 us -> 9.07 us
    dot_general x18 -> x0, matrix products: 4.33 us -> none  [the longest x3 0.87 us: block_scores(): jnp.einsum('qhe,ke->hqk', queries, key_block[:, :head_dim], preferred_ele...]
    convert_element_type x5 -> x0, local copies, waits for them, and re-layouts: 2.06 us -> none  [the longest x2 0.72 us: shards(): resp_out = r_output.reshape(1, resp_rows, query_width).astype(jnp.bfloat16)]
  transfers between devices with their start and end apart: 2 -> 0, of which waited for: 2 -> 0; matrix products, arithmetic and copies ran while one was open for 8% -> 0% of each run, Pallas kernels for 0% -> 0%
where the time goes in v1:
time: 33.3 us; the launch traced here: 32.7 us
  Pallas kernels  23 us (69%)
  local copies, waits for them, and re-layouts  9.07 us (27%)
  between operations  0.66 us (2%)
    pallas_call x1, Pallas kernels, shards(): pl.pallas_call(functools.partial(kernel, nz, nx, ns), out_shape=[like(a.s...  23 us
    unnamed x20, local copies, waits for them, and re-layouts  9.07 us

profile of v1, /device:TPU:1, one launch (start us, length us, event | category | flops | bytes accessed | tf_op | source)
XLA Modules:
  0.0 32.7 jit_solution(8316864346941356103)
XLA Ops:
  0.6 0.0 copy-start
  0.6 0.8 %copy-done = bf16[1,64,512]{2,1,0:T(8,128)(2,1)S(1)} copy-done((bf16[1,64,512]{2,1,0:T(8,128)(2,1)S(1)}, bf16[1,64,512]{2,1,0:T(8,128)(2,1)}, u32[]{:S(2)}) %copy-start) | copy-done | bytes 65560
  1.5 0.0 copy-start.1
  1.5 0.8 %copy-done.1 = bf16[1,64,512]{2,1,0:T(8,128)(2,1)S(1)} copy-done((bf16[1,64,512]{2,1,0:T(8,128)(2,1)S(1)}, bf16[1,64,512]{2,1,0:T(8,128)(2,1)}, u32[]{:S(2)}) %copy-start.1) | copy-done | bytes 65560
  2.3 0.0 copy-start.2
  2.3 0.8 %copy-done.2 = bf16[64,256]{1,0:T(8,128)(2,1)S(1)} copy-done((bf16[64,256]{1,0:T(8,128)(2,1)S(1)}, bf16[64,256]{1,0:T(8,128)(2,1)}, u32[]{:S(2)}) %copy-start.2) | copy-done | bytes 32792
  3.1 0.0 copy-start.3
  3.1 0.8 %copy-done.3 = bf16[64,256]{1,0:T(8,128)(2,1)S(1)} copy-done((bf16[64,256]{1,0:T(8,128)(2,1)S(1)}, bf16[64,256]{1,0:T(8,128)(2,1)}, u32[]{:S(2)}) %copy-start.3) | copy-done | bytes 32792
  3.8 0.0 copy-start.4
  3.8 0.8 %copy-done.4 = bf16[64,256]{1,0:T(8,128)(2,1)S(1)} copy-done((bf16[64,256]{1,0:T(8,128)(2,1)S(1)}, bf16[64,256]{1,0:T(8,128)(2,1)}, u32[]{:S(2)}) %copy-start.4) | copy-done | bytes 32792
  4.6 0.0 copy-start.5
  4.6 0.8 %copy-done.5 = bf16[1,64,256]{2,1,0:T(8,128)(2,1)S(1)} copy-done((bf16[1,64,256]{2,1,0:T(8,128)(2,1)S(1)}, bf16[1,64,256]{2,1,0:T(8,128)(2,1)}, u32[]{:S(2)}) %copy-start.5) | copy-done | bytes 32792
  5.3 0.0 copy-start.6
  5.4 0.7 %copy-done.6 = s32[4]{0:T(128)S(1)} copy-done((s32[4]{0:T(128)S(1)}, s32[4]{0:T(128)}, u32[]{:S(2)}) %copy-start.6) | copy-done | bytes 40
  6.0 23.0 %shard_map.118 = (bf16[64,256]{1,0:T(8,128)(2,1)S(1)}, bf16[1,64,512]{2,1,0:T(8,128)(2,1)S(1)}, bf16[64,256]{1,0:T(8,128)(2,1)S(1)}, bf16[1,64,512]{2,1,0:T(8,12...) custom-call(s32[4]{0:T(128)S(1)} %copy-done.6, bf16[64,256]{1,0:T(8,128)(2,1)S(1)} %copy-done.2, ...), custom_call_target="tpu_custom_call" | custom-call | tf_op jit(solution)/shard_map/pallas_call | solution.py:372
  29.0 0.6 %copy.19 = bf16[64,256]{1,0:T(8,128)(2,1)} copy(bf16[64,256]{1,0:T(8,128)(2,1)S(1)} %get-tuple-element.12) | data formatting | bytes 65536
  29.6 0.6 %copy.20 = bf16[1,64,512]{2,1,0:T(8,128)(2,1)} copy(bf16[1,64,512]{2,1,0:T(8,128)(2,1)S(1)} %get-tuple-element.13) | data formatting | bytes 131072
  30.2 0.6 %copy.21 = bf16[64,256]{1,0:T(8,128)(2,1)} copy(bf16[64,256]{1,0:T(8,128)(2,1)S(1)} %get-tuple-element.14) | data formatting | bytes 65536
  30.9 0.6 %copy.22 = bf16[1,64,512]{2,1,0:T(8,128)(2,1)} copy(bf16[1,64,512]{2,1,0:T(8,128)(2,1)S(1)} %get-tuple-element.15) | data formatting | bytes 131072
  31.5 0.6 %copy.23 = bf16[64,256]{1,0:T(8,128)(2,1)} copy(bf16[64,256]{1,0:T(8,128)(2,1)S(1)} %get-tuple-element.16) | data formatting | bytes 65536
  32.1 0.6 %copy.24 = bf16[1,64,256]{2,1,0:T(8,128)(2,1)} copy(bf16[1,64,256]{2,1,0:T(8,128)(2,1)S(1)} %get-tuple-element.17) | data formatting | bytes 65536
Async XLA Ops:
  0.6 0.8 %copy-start = (bf16[1,64,512]{2,1,0:T(8,128)(2,1)S(1)}, bf16[1,64,512]{2,1,0:T(8,128)(2,1)}, u32[]{:S(2)}) copy-start(bf16[1,64,512]{2,1,0:T(8,128)(2,1)} %rq.1) | copy-start | bytes 196612
  1.5 0.8 %copy-start.1 = (bf16[1,64,512]{2,1,0:T(8,128)(2,1)S(1)}, bf16[1,64,512]{2,1,0:T(8,128)(2,1)}, u32[]{:S(2)}) copy-start(bf16[1,64,512]{2,1,0:T(8,128)(2,1)} %rdo.1) | copy-start | bytes 196612
  2.3 0.8 %copy-start.2 = (bf16[64,256]{1,0:T(8,128)(2,1)S(1)}, bf16[64,256]{1,0:T(8,128)(2,1)}, u32[]{:S(2)}) copy-start(bf16[64,256]{1,0:T(8,128)(2,1)} %pq.1) | copy-start | bytes 98308
  3.1 0.8 %copy-start.3 = (bf16[64,256]{1,0:T(8,128)(2,1)S(1)}, bf16[64,256]{1,0:T(8,128)(2,1)}, u32[]{:S(2)}) copy-start(bf16[64,256]{1,0:T(8,128)(2,1)} %pkv.1) | copy-start | bytes 98308
  3.8 0.8 %copy-start.4 = (bf16[64,256]{1,0:T(8,128)(2,1)S(1)}, bf16[64,256]{1,0:T(8,128)(2,1)}, u32[]{:S(2)}) copy-start(bf16[64,256]{1,0:T(8,128)(2,1)} %pdo.1) | copy-start | bytes 98308
  4.6 0.8 %copy-start.5 = (bf16[1,64,256]{2,1,0:T(8,128)(2,1)S(1)}, bf16[1,64,256]{2,1,0:T(8,128)(2,1)}, u32[]{:S(2)}) copy-start(bf16[1,64,256]{2,1,0:T(8,128)(2,1)} %rkv.1) | copy-start | bytes 98308
  5.3 0.7 %copy-start.6 = (s32[4]{0:T(128)S(1)}, s32[4]{0:T(128)}, u32[]{:S(2)}) copy-start(s32[4]{0:T(128)} %lens.1) | copy-start | bytes 52

commit v2 on v1

--- a/solution.py
+++ b/solution.py
@@ -37,8 +37,8 @@
 
 
 def kernel(
-    nz, nx, ns, lens, pq, pkv, pdo, rq, rkv, rdo, po, ro, pdq, rdq, pdkv, rdkv,
-    pk, rk, qa, da, sp, gp, so, go, wp, dp, wo, do, away, got, mine, rs, oway, rr, fin,
+    nz, nx, ns, lens_in, pq, pkv, pdo, rq, rkv, rdo, po, ro, pdq, rdq, pdkv, rdkv,
+    pk, rk, qa, da, sp, gp, so, go, wp, dp, wo, do, away, got, mine, rs, oway, rr, fin, lens, in_sem,
     g_send, g_recv, f_send, f_recv, r_send, r_recv, p_sem, s_send, s_recv, q_send, q_recv, e_sem,
 ):
     n = nz * nx
@@ -79,9 +79,18 @@
     loop(1, n, greet)
     pl.semaphore_signal(barrier, inc=1, device_id=sib, device_id_type=MESH)
 
-    for k in range(2):
-        pk[k * n + me] = pkv[k * half : (k + 1) * half, :]
-    rk[z] = rkv[0]
+    moves = [(pkv.at[k * half : (k + 1) * half], pk.at[k * n + me]) for k in range(2)]
+    moves += [(rkv.at[0], rk.at[z])]
+    for to, resp_in, prompt_in in ((qa, rq, pq), (da, rdo, pdo)):
+        for k in range(r_heads):
+            moves.append((resp_in.at[0, :, k * e : (k + 1) * e], to.at[k * r_rows : (k + 1) * r_rows]))
+        for k in range(p_heads):
+            first = rc + k * rows
+            moves.append((prompt_in.at[:, k * e : (k + 1) * e], to.at[first : first + rows]))
+    moves.append((lens_in, lens))
+    moves = [pltpu.make_async_copy(a, b, in_sem.at[k]) for k, (a, b) in enumerate(moves)]
+    for move in moves:
+        move.start()
 
     def blank(i):
         @pl.when(i > z)
@@ -89,23 +98,17 @@
             rk[i] = jnp.zeros(rk.shape[1:], bf16)
 
     loop(0, nz, blank)
-    for k in range(r_heads):
-        qa[k * r_rows : (k + 1) * r_rows, :] = rq[0, :, k * e : (k + 1) * e]
-        da[k * r_rows : (k + 1) * r_rows, :] = rdo[0, :, k * e : (k + 1) * e]
-    for k in range(p_heads):
-        qa[rc + k * rows : rc + (k + 1) * rows, :] = pq[:, k * e : (k + 1) * e]
-        da[rc + k * rows : rc + (k + 1) * rows, :] = pdo[:, k * e : (k + 1) * e]
 
     pl.semaphore_wait(barrier, n)
 
     def gather(c, src):
-        return copy(pk.at[h * n + src], pk.at[h * n + src], g_send.at[c], g_recv.at[src], chip(c))
+        return copy(pkv.at[pl.ds(pl.multiple_of(h * half, half), half)], pk.at[h * n + src], g_send.at[c], g_recv.at[src], chip(c))
 
     def pass_on(c, k):
         return copy(pk.at[k * n + c], pk.at[k * n + c], f_send.at[c], f_recv.at[c], sib)
 
     def resp(to, src):
-        return copy(rk.at[src], rk.at[src], r_send.at[to], r_recv.at[src], {"seq": to})
+        return copy(rkv.at[0], rk.at[src], r_send.at[to], r_recv.at[src], {"seq": to})
 
     loop(1, n, lambda d: gather((me + d) % n, me).start())
 
@@ -115,6 +118,8 @@
             resp(i, z).start()
 
     loop(0, nz, resp_start)
+    for move in moves:
+        move.wait()
 
     def forward(d):
         c = (me + n - d) % n
@@ -155,7 +160,7 @@
         s_p = jnp.where(key <= at, s[:, rc:], floor_score)
         sp[i, :, :rc] = s_r
         sp[i, :, rc:] = s_p
-        gp[i] = dot(kv[:, e:], da[...], NT)
+        gp[i] = dot(kv[:, e:], da[...], NT).astype(gp.dtype)
         return (
             jnp.maximum(top_r, jnp.max(s_r, axis=0, keepdims=True)),
             jnp.maximum(top_p, jnp.max(s_p, axis=0, keepdims=True)),
@@ -179,7 +184,7 @@
         sp[i] = ex
         return (
             total + jnp.sum(ex, axis=0, keepdims=True),
-            delta + jnp.sum(ex * gp[i], axis=0, keepdims=True),
+            delta + jnp.sum(ex * gp[i].astype(f32), axis=0, keepdims=True),
         )
 
     zero_r, zero_a = jnp.zeros((1, rc), f32), jnp.zeros((1, rc + pc), f32)
@@ -196,7 +201,7 @@
     def weigh(i, carry):
         prob = sp[i] * share
         wp[i] = prob.astype(bf16)
-        dp[i] = (prob * (gp[i] - delta)).astype(bf16)
+        dp[i] = (prob * (gp[i].astype(f32) - delta)).astype(bf16)
         return carry
 
     def own_weigh(i, carry):
@@ -327,6 +332,16 @@
     loop(0, nz, sent)
     pair.wait_send()
     last.wait_send()
+
+
+def hand_over(*refs):
+    sem = refs[-1]
+    half = len(refs) // 2
+    moves = [pltpu.make_async_copy(refs[k], refs[half + k], sem.at[k]) for k in range(half)]
+    for move in moves:
+        move.start()
+    for move in moves:
+        move.wait()
 
 
 def shards(nz, nx, ns, prompt_q, prompt_kv, prompt_dout, resp_q, resp_kv, resp_dout, resp_lengths):
@@ -350,7 +365,7 @@
         ((qc, e), bf16),
         ((qc, e), bf16),
         ((nb2, bk, qc), f32),
-        ((nb2, bk, qc), f32),
+        ((nb2, bk, qc), f32 if n <= 32 else bf16),
         ((no, bo, rc), f32),
         ((no, bo, rc), f32),
         ((nb2, bk, qc), bf16),
@@ -367,21 +382,30 @@
     ]
     room = sum(math.prod(s) * jnp.dtype(t).itemsize for s, t in scratch)
     dma = pltpu.SemaphoreType.DMA
-    sems = [dma((k,)) for k in (n, n, n, n, nz, nz, 2, n, n, nz, nz, 2)]
+    heads = qc // rows
+    sems = [pltpu.SMEM(resp_lengths.shape, jnp.int32)]
+    sems += [dma((k,)) for k in (2 * heads + 4, n, n, n, n, nz, nz, 2, n, n, nz, nz, 2)]
     like = jax.ShapeDtypeStruct
-    return pl.pallas_call(
+    results = pl.pallas_call(
         functools.partial(kernel, nz, nx, ns),
         out_shape=[
-            like(a.shape, bf16)
+            pltpu.VMEM(a.shape, bf16)
             for a in (prompt_q, resp_q, prompt_q, resp_q, prompt_kv, resp_kv)
         ],
-        in_specs=[pl.BlockSpec(memory_space=pltpu.SMEM)] + [vmem] * 6,
+        in_specs=[pl.BlockSpec(memory_space=pltpu.HBM)] * 7,
         out_specs=[vmem] * 6,
         scratch_shapes=[pltpu.VMEM(s, t) for s, t in scratch] + sems,
         compiler_params=pltpu.CompilerParams(
-            collective_id=0, has_side_effects=True, vmem_limit_bytes=room + 8 * 2**20
+            collective_id=0, has_side_effects=True, vmem_limit_bytes=max(56 * 2**20, room + 3 * 2**20)
         ),
     )(resp_lengths, prompt_q, prompt_kv, prompt_dout, resp_q, resp_kv, resp_dout)
+    return pl.pallas_call(
+        hand_over,
+        out_shape=[like(a.shape, a.dtype) for a in results],
+        in_specs=[pl.BlockSpec(memory_space=pl.ANY)] * 6,
+        out_specs=[pl.BlockSpec(memory_space=pltpu.HBM)] * 6,
+        scratch_shapes=[dma((6,))],
+    )(*results)
 
 
 def solution(mesh):

time: 33.3 us -> 36.5 us (1.096)
  Pallas kernels: 23 us -> 31.9 us
  local copies, waits for them, and re-layouts: 9.07 us -> 3.68 us
    pallas_call x1 -> x2, Pallas kernels: 23 us -> 31.9 us  [the longest x1 22.8 us: shards(): pl.pallas_call(functools.partial(kernel, nz, nx, ns), out_shape=[pltpu.VM...]
    unnamed x20 -> x12, local copies, waits for them, and re-layouts: 9.07 us -> 3.68 us
where the time goes in v2:
time: 36.5 us; the launch traced here: 36.3 us
  Pallas kernels  31.9 us (87%)
  local copies, waits for them, and re-layouts  3.68 us (10%)
  between operations  0.66 us (2%)
    pallas_call x1, Pallas kernels, shards(): pl.pallas_call(functools.partial(kernel, nz, nx, ns), out_shape=[pltpu.VM...  22.8 us
    pallas_call x1, Pallas kernels, shards(): pl.pallas_call(hand_over, out_shape=[like(a.shape, a.dtype) for a in resu...  9.09 us
    unnamed x12, local copies, waits for them, and re-layouts  3.68 us

profile of v2, /device:TPU:1, one launch (start us, length us, event | category | flops | bytes accessed | tf_op | source)
XLA Modules:
  0.0 36.3 jit_solution(9155608400010660526)
XLA Ops:
  0.6 22.8 %shard_map.118 = (bf16[64,256]{1,0:T(8,128)(2,1)S(1)}, bf16[1,64,512]{2,1,0:T(8,128)(2,1)S(1)}, bf16[64,256]{1,0:T(8,128)(2,1)S(1)}, bf16[1,64,512]{2,1,0:T(8,12...) custom-call(s32[4]{0:T(128)} %lens_in.1, bf16[64,256]{1,0:T(8,128)(2,1)} %pq.1, ...), custom_call_target="tpu_custom_call" | custom-call | tf_op jit(solution)/shard_map/pallas_call | solution.py:389
  23.5 0.0 copy-start
  23.5 0.6 %copy-done = bf16[1,64,512]{2,1,0:T(8,128)(2,1)} copy-done((bf16[1,64,512]{2,1,0:T(8,128)(2,1)}, bf16[1,64,512]{2,1,0:T(8,128)(2,1)S(1)}, u32[]{:S(2)}) %copy-start) | copy-done | bytes 65560
  24.1 0.0 copy-start.1
  24.1 0.6 %copy-done.1 = bf16[1,64,512]{2,1,0:T(8,128)(2,1)} copy-done((bf16[1,64,512]{2,1,0:T(8,128)(2,1)}, bf16[1,64,512]{2,1,0:T(8,128)(2,1)S(1)}, u32[]{:S(2)}) %copy-start.1) | copy-done | bytes 65560
  24.7 0.0 copy-start.2
  24.7 0.6 %copy-done.2 = bf16[64,256]{1,0:T(8,128)(2,1)} copy-done((bf16[64,256]{1,0:T(8,128)(2,1)}, bf16[64,256]{1,0:T(8,128)(2,1)S(1)}, u32[]{:S(2)}) %copy-start.2) | copy-done | bytes 32792
  25.3 0.0 copy-start.3
  25.3 0.6 %copy-done.3 = bf16[64,256]{1,0:T(8,128)(2,1)} copy-done((bf16[64,256]{1,0:T(8,128)(2,1)}, bf16[64,256]{1,0:T(8,128)(2,1)S(1)}, u32[]{:S(2)}) %copy-start.3) | copy-done | bytes 32792
  25.9 0.0 copy-start.4
  25.9 0.6 %copy-done.4 = bf16[64,256]{1,0:T(8,128)(2,1)} copy-done((bf16[64,256]{1,0:T(8,128)(2,1)}, bf16[64,256]{1,0:T(8,128)(2,1)S(1)}, u32[]{:S(2)}) %copy-start.4) | copy-done | bytes 32792
  26.6 0.0 copy-start.5
  26.6 0.6 %copy-done.5 = bf16[1,64,256]{2,1,0:T(8,128)(2,1)} copy-done((bf16[1,64,256]{2,1,0:T(8,128)(2,1)}, bf16[1,64,256]{2,1,0:T(8,128)(2,1)S(1)}, u32[]{:S(2)}) %copy-start.5) | copy-done | bytes 32792
  27.2 9.1 %shard_map.119 = (bf16[64,256]{1,0:T(8,128)(2,1)}, bf16[1,64,512]{2,1,0:T(8,128)(2,1)}, bf16[64,256]{1,0:T(8,128)(2,1)}, bf16[1,64,512]{2,1,0:T(8,128)(2,1)}, bf...) custom-call(bf16[64,256]{1,0:T(8,128)(2,1)} %copy-done.2, bf16[1,64,512]{2,1,0:T(8,128)(2,1)} %copy-done, ...), custom_call_target="tpu_custom_call" | custom-call | tf_op jit(solution)/shard_map/pallas_call | solution.py:402
Async XLA Ops:
  23.5 0.6 %copy-start = (bf16[1,64,512]{2,1,0:T(8,128)(2,1)}, bf16[1,64,512]{2,1,0:T(8,128)(2,1)S(1)}, u32[]{:S(2)}) copy-start(bf16[1,64,512]{2,1,0:T(8,128)(2,1)S(1)} %get-tuple-element.13.refs_1_) | copy-start | bytes 196612
  24.1 0.6 %copy-start.1 = (bf16[1,64,512]{2,1,0:T(8,128)(2,1)}, bf16[1,64,512]{2,1,0:T(8,128)(2,1)S(1)}, u32[]{:S(2)}) copy-start(bf16[1,64,512]{2,1,0:T(8,128)(2,1)S(1)} %get-tuple-element.15.refs_3_) | copy-start | bytes 196612
  24.7 0.6 %copy-start.2 = (bf16[64,256]{1,0:T(8,128)(2,1)}, bf16[64,256]{1,0:T(8,128)(2,1)S(1)}, u32[]{:S(2)}) copy-start(bf16[64,256]{1,0:T(8,128)(2,1)S(1)} %get-tuple-element.12.refs_0_) | copy-start | bytes 98308
  25.3 0.6 %copy-start.3 = (bf16[64,256]{1,0:T(8,128)(2,1)}, bf16[64,256]{1,0:T(8,128)(2,1)S(1)}, u32[]{:S(2)}) copy-start(bf16[64,256]{1,0:T(8,128)(2,1)S(1)} %get-tuple-element.14.refs_2_) | copy-start | bytes 98308
  25.9 0.6 %copy-start.4 = (bf16[64,256]{1,0:T(8,128)(2,1)}, bf16[64,256]{1,0:T(8,128)(2,1)S(1)}, u32[]{:S(2)}) copy-start(bf16[64,256]{1,0:T(8,128)(2,1)S(1)} %get-tuple-element.16.refs_4_) | copy-start | bytes 98308
  26.6 0.6 %copy-start.5 = (bf16[1,64,256]{2,1,0:T(8,128)(2,1)}, bf16[1,64,256]{2,1,0:T(8,128)(2,1)S(1)}, u32[]{:S(2)}) copy-start(bf16[1,64,256]{2,1,0:T(8,128)(2,1)S(1)} %get-tuple-element.17.refs_5_) | copy-start | bytes 98308

commit v3 on v2

--- a/solution.py
+++ b/solution.py
@@ -243,7 +243,6 @@
         def _():
             back(i, z).start()
 
-    loop(0, nz, back_start)
 
     def my_part(b, carry):
         mine[b] = part(h, b)
@@ -263,6 +262,7 @@
         return copy(rs.at[0, c], rs.at[1, src], s_send.at[c], s_recv.at[src], chip(c))
 
     loop(1, n, lambda d: scatter((me + d) % n, me).start())
+    loop(0, nz, back_start)
     rs[1, me] = rs[0, me]
 
     def out_own(i, carry):
@@ -402,9 +402,10 @@
     return pl.pallas_call(
         hand_over,
         out_shape=[like(a.shape, a.dtype) for a in results],
-        in_specs=[pl.BlockSpec(memory_space=pl.ANY)] * 6,
+        in_specs=[vmem] * 6,
         out_specs=[pl.BlockSpec(memory_space=pltpu.HBM)] * 6,
         scratch_shapes=[dma((6,))],
+        compiler_params=pltpu.CompilerParams(vmem_limit_bytes=4 * 2**20),
     )(*results)
 
 

time: 36.5 us -> 24.3 us (0.67)
  Pallas kernels: 31.9 us -> 23.4 us
  local copies, waits for them, and re-layouts: 3.68 us -> 0 us
    pallas_call x1, Pallas kernels: 9.09 us -> 0.75 us  [shards(): pl.pallas_call(hand_over, out_shape=[like(a.shape, a.dtype) for a in resu...]
    unnamed x12 -> x0, local copies, waits for them, and re-layouts: 3.68 us -> none
where the time goes in v3:
time: 24.3 us; the launch traced here: 24.1 us
  Pallas kernels  23.4 us (96%)
  between operations  0.64 us (3%)
    pallas_call x1, Pallas kernels, shards(): pl.pallas_call(functools.partial(kernel, nz, nx, ns), out_shape=[pltpu.VM...  22.7 us
    pallas_call x1, Pallas kernels, shards(): pl.pallas_call(hand_over, out_shape=[like(a.shape, a.dtype) for a in resu...  0.75 us

profile of v3, /device:TPU:1, one launch (start us, length us, event | category | flops | bytes accessed | tf_op | source)
XLA Modules:
  0.0 24.1 jit_solution(6725242342615394824)
XLA Ops:
  0.6 22.7 %shard_map.118 = (bf16[64,256]{1,0:T(8,128)(2,1)S(1)}, bf16[1,64,512]{2,1,0:T(8,128)(2,1)S(1)}, bf16[64,256]{1,0:T(8,128)(2,1)S(1)}, bf16[1,64,512]{2,1,0:T(8,12...) custom-call(s32[4]{0:T(128)} %lens_in.1, bf16[64,256]{1,0:T(8,128)(2,1)} %pq.1, ...), custom_call_target="tpu_custom_call" | custom-call | tf_op jit(solution)/shard_map/pallas_call | solution.py:389
  23.3 0.7 %shard_map.119 = (bf16[64,256]{1,0:T(8,128)(2,1)}, bf16[1,64,512]{2,1,0:T(8,128)(2,1)}, bf16[64,256]{1,0:T(8,128)(2,1)}, bf16[1,64,512]{2,1,0:T(8,128)(2,1)}, bf...) custom-call(bf16[64,256]{1,0:T(8,128)(2,1)S(1)} %get-tuple-element.12.refs_0_, ...), custom_call_target="tpu_custom_call" | custom-call | tf_op jit(solution)/shard_map/pallas_call | solution.py:402

commit v4 on v3

--- a/solution.py
+++ b/solution.py
@@ -128,25 +128,6 @@
 
     loop(1, n, forward)
 
-    def resp_wait(i):
-        @pl.when(i < z)
-        def _():
-            resp(i, i).wait_recv()
-
-    loop(0, nz, resp_wait)
-
-    def own_scores(i, top):
-        kv = rk[pl.ds(i * zpb, zpb)].reshape(bo, kvw)
-        s = dot(kv[:, :e], qa[:rc], NT) * scale2
-        key = i * bo + lax.broadcasted_iota(jnp.int32, (bo, rc), 0)
-        at = z * r_rows + lax.broadcasted_iota(jnp.int32, (bo, rc), 1) % r_rows
-        s = jnp.where(key <= at, s, floor_score)
-        so[i] = s
-        go[i] = dot(kv[:, e:], da[:rc], NT)
-        return jnp.maximum(top, jnp.max(s, axis=0, keepdims=True))
-
-    top_r = fold(no, own_scores, jnp.full((1, rc), floor_score, f32))
-
     loop(1, n, lambda d: pass_on((me + d) % n, 1 - h).wait_recv())
 
     def scores(i, tops):
@@ -166,7 +147,26 @@
             jnp.maximum(top_p, jnp.max(s_p, axis=0, keepdims=True)),
         )
 
-    top_r, top_p = fold(nb2, scores, (top_r, jnp.full((1, pc), floor_score, f32)))
+    top_r, top_p = fold(nb2, scores, (jnp.full((1, rc), floor_score, f32), jnp.full((1, pc), floor_score, f32)))
+    def resp_wait(i):
+        @pl.when(i < z)
+        def _():
+            resp(i, i).wait_recv()
+
+    loop(0, nz, resp_wait)
+
+    def own_scores(i, top):
+        kv = rk[pl.ds(i * zpb, zpb)].reshape(bo, kvw)
+        s = dot(kv[:, :e], qa[:rc], NT) * scale2
+        key = i * bo + lax.broadcasted_iota(jnp.int32, (bo, rc), 0)
+        at = z * r_rows + lax.broadcasted_iota(jnp.int32, (bo, rc), 1) % r_rows
+        s = jnp.where(key <= at, s, floor_score)
+        so[i] = s
+        go[i] = dot(kv[:, e:], da[:rc], NT)
+        return jnp.maximum(top, jnp.max(s, axis=0, keepdims=True))
+
+    top_r = fold(no, own_scores, top_r)
+
     top = jnp.concatenate([top_r, top_p], axis=1)
 
     def own_exp(i, sums):

time: 24.3 us -> 23.8 us (0.979)
  Pallas kernels: 23.4 us -> 23 us
    pallas_call x1, Pallas kernels: 22.7 us -> 22.3 us  [shards(): pl.pallas_call(functools.partial(kernel, nz, nx, ns), out_shape=[pltpu.VM...]
where the time goes in v4:
time: 23.8 us; the launch traced here: 23.7 us
  Pallas kernels  23 us (97%)
  between operations  0.64 us (3%)
    pallas_call x1, Pallas kernels, shards(): pl.pallas_call(functools.partial(kernel, nz, nx, ns), out_shape=[pltpu.VM...  22.3 us
    pallas_call x1, Pallas kernels, shards(): pl.pallas_call(hand_over, out_shape=[like(a.shape, a.dtype) for a in resu...  0.75 us

profile of v4, /device:TPU:1, one launch (start us, length us, event | category | flops | bytes accessed | tf_op | source)
XLA Modules:
  0.0 23.7 jit_solution(11404931617042800212)
XLA Ops:
  0.6 22.3 %shard_map.118 = (bf16[64,256]{1,0:T(8,128)(2,1)S(1)}, bf16[1,64,512]{2,1,0:T(8,128)(2,1)S(1)}, bf16[64,256]{1,0:T(8,128)(2,1)S(1)}, bf16[1,64,512]{2,1,0:T(8,12...) custom-call(s32[4]{0:T(128)} %lens_in.1, bf16[64,256]{1,0:T(8,128)(2,1)} %pq.1, ...), custom_call_target="tpu_custom_call" | custom-call | tf_op jit(solution)/shard_map/pallas_call | solution.py:389
  22.9 0.7 %shard_map.119 = (bf16[64,256]{1,0:T(8,128)(2,1)}, bf16[1,64,512]{2,1,0:T(8,128)(2,1)}, bf16[64,256]{1,0:T(8,128)(2,1)}, bf16[1,64,512]{2,1,0:T(8,128)(2,1)}, bf...) custom-call(bf16[64,256]{1,0:T(8,128)(2,1)S(1)} %get-tuple-element.12.refs_0_, ...), custom_call_target="tpu_custom_call" | custom-call | tf_op jit(solution)/shard_map/pallas_call | solution.py:402
